TPU v7x, 128 devices: a whole 4x4x4 slice. The times are simulated.
128 devices in a mesh: sym: 8 (over y_hi, x), tile: 8 (over z, y_lo), occ: 2 (over core).
Axes of the slice: x: 4, y: 4 (y_hi: 2, y_lo: 2; y = y_hi * 2 + y_lo), z: 4, core: 2. Of those that a mesh axis runs over, the one named last changes fastest.
Arguments:
- irrep_dims: int32 [8], replicated, may hold values from 1 to 384, 1600 in all
- chol_vectors: bfloat16 [16, 3072, 384], P(('sym', 'occ'), 'tile'), may hold values from -0.375 to 0.375
- amplitudes: bfloat16 [8, 16, 3072, 384], P('sym', 'occ', 'tile'), may hold values from -6 to 6
Outputs:
- sigma_ladder: float32 [8, 16, 3072, 384], P('sym', 'occ', 'tile')
Inputs may be any that keep to these rules, and one draw needn't show every extreme that they name: irrep_dims[h] is the number of virtual orbitals of irrep h; the entries sum to 1600 and the largest is exactly 384.
All inputs are finite; a program needn't handle non-finite values.
Results may differ from a plain program's by a relative error of at most 0.0029.
Values may be sent and summed in bfloat16 or wider, within the bound.
A program may use at most 128 MiB of HBM per device.

v0:
```python
import functools

import jax
import jax.numpy as jnp
from jax import lax
from jax.experimental import pallas as pl
from jax.experimental.pallas import tpu as pltpu
from jax.sharding import PartitionSpec as P

MESH = pl.DeviceIdType.MESH
V = 384
NI = 8
PIECES = 2
PV = V // PIECES
STEPS = 4
CROSSF, OWN, PASS_Z, FWD_Y, PASS_Y, PAR = range(6)
SEQUENCE = (
    (1, 0, 0),
    (1, 0, 2),
    (1, 0, 3),
    (1, 0, 1),
    (2, 0, 0),
    (1, 1, 0),
    (2, 1, 0),
    (1, 1, 1),
    (1, 1, 3),
    (2, 0, 3),
    (2, 0, 1),
    (2, 1, 1),
    (2, 1, 3),
    (2, 0, 2),
    (1, 1, 2),
    (2, 1, 2),
)
EVENTS = {
    0: (
        (4, ((CROSSF, 0), (CROSSF, 1), (OWN, 0, 1, 0), (OWN, 0, 3, 0), (PASS_Z, 0, 0), (PASS_Z, 0, 1), (OWN, 0, 1, 1), (OWN, 0, 3, 1), (OWN, 1, 0, 0), (OWN, 1, 0, 1), (PASS_Z, 1, 0), (PASS_Z, 3, 0), (OWN, 0, 2, 0), (OWN, 0, 2, 1), (FWD_Y, 0, 1), (PAR, 0, 0, 1), (FWD_Y, 0, 0), (PAR, 0, 0, 0),)),
        (6, ((OWN, 1, 1, 0),)),
        (8, ((PASS_Z, 1, 1), (PASS_Z, 3, 1),)),
        (9, ((PASS_Y, 0, 1), (PASS_Y, 0, 0),)),
        (10, ((OWN, 1, 1, 1),)),
        (12, ((OWN, 1, 3, 0), (FWD_Y, 1, 0), (FWD_Y, 3, 0), (PAR, 0, 1, 0), (PAR, 0, 3, 0),)),
        (15, ((PAR, 1, 0, 0), (PAR, 1, 0, 1),)),
        (16, ((OWN, 1, 2, 1), (PASS_Z, 2, 0), (PASS_Z, 2, 1),)),
        (19, ((PASS_Y, 1, 0), (PASS_Y, 3, 0),)),
        (20, ((OWN, 1, 2, 0), (FWD_Y, 1, 1), (FWD_Y, 3, 1), (PAR, 0, 1, 1), (PAR, 0, 3, 1),)),
        (25, ((FWD_Y, 2, 0), (FWD_Y, 2, 1), (PAR, 0, 2, 0), (PAR, 0, 2, 1), (PAR, 1, 3, 0), (PAR, 1, 1, 0),)),
        (28, ((OWN, 1, 3, 1), (PASS_Y, 3, 1), (PASS_Y, 1, 1),)),
        (33, ((PASS_Y, 2, 0), (PASS_Y, 2, 1),)),
        (37, ((PAR, 1, 3, 1), (PAR, 1, 1, 1),)),
        (41, ((PAR, 1, 2, 0), (PAR, 1, 2, 1),)),
    ),
    1: (
        (4, ((CROSSF, 0), (OWN, 0, 1, 0), (OWN, 0, 3, 0), (PASS_Z, 0, 0), (PASS_Z, 0, 1), (OWN, 0, 1, 1), (OWN, 0, 3, 1), (CROSSF, 1), (PASS_Z, 1, 0), (PASS_Z, 3, 0), (OWN, 0, 2, 0), (OWN, 0, 2, 1), (FWD_Y, 0, 1), (FWD_Y, 0, 0),)),
        (5, ((OWN, 1, 0, 0),)),
        (6, ((OWN, 1, 1, 0),)),
        (7, ((OWN, 1, 3, 0),)),
        (8, ((PASS_Z, 1, 1), (PASS_Z, 3, 1),)),
        (9, ((PAR, 0, 0, 1), (PAR, 1, 0, 1),)),
        (10, ((OWN, 1, 1, 1),)),
        (11, ((OWN, 1, 3, 1),)),
        (12, ((FWD_Y, 1, 0), (FWD_Y, 3, 0),)),
        (13, ((PAR, 0, 0, 0), (PAR, 1, 0, 0),)),
        (15, ((OWN, 1, 2, 0),)),
        (16, ((OWN, 1, 2, 1), (PASS_Z, 2, 0), (PASS_Z, 2, 1),)),
        (18, ((PAR, 0, 1, 0), (PAR, 1, 1, 0),)),
        (20, ((FWD_Y, 1, 1), (FWD_Y, 3, 1), (OWN, 1, 0, 1),)),
        (22, ((PAR, 0, 3, 0), (PAR, 1, 3, 0),)),
        (24, ((FWD_Y, 2, 0), (FWD_Y, 2, 1),)),
        (26, ((PAR, 0, 1, 1), (PAR, 1, 1, 1),)),
        (30, ((PAR, 1, 3, 1),)),
        (31, ((PAR, 0, 3, 1),)),
        (35, ((PAR, 0, 2, 0), (PAR, 1, 2, 0),)),
        (39, ((PAR, 0, 2, 1), (PAR, 1, 2, 1),)),
    ),
    2: (
        (4, ((CROSSF, 0), (CROSSF, 1), (OWN, 0, 1, 0), (OWN, 0, 3, 0), (FWD_Y, 0, 0), (PAR, 0, 0, 0), (OWN, 0, 1, 1), (OWN, 0, 3, 1), (PAR, 0, 0, 1), (FWD_Y, 0, 1), (OWN, 1, 0, 0), (OWN, 1, 0, 1), (OWN, 0, 2, 0), (PAR, 0, 1, 0), (FWD_Y, 1, 0), (OWN, 0, 2, 1), (PASS_Y, 0, 0), (PASS_Y, 0, 1),)),
        (6, ((FWD_Y, 3, 0), (PAR, 0, 3, 0),)),
        (7, ((OWN, 1, 3, 0),)),
        (8, ((PASS_Y, 1, 0),)),
        (9, ((PAR, 1, 0, 0),)),
        (10, ((FWD_Y, 1, 1), (PAR, 0, 1, 1),)),
        (11, ((OWN, 1, 1, 0), (OWN, 1, 3, 1),)),
        (12, ((PAR, 1, 0, 1),)),
        (13, ((PASS_Y, 3, 0),)),
        (14, ((FWD_Y, 3, 1), (PAR, 0, 3, 1),)),
        (15, ((OWN, 1, 2, 0),)),
        (16, ((PAR, 1, 1, 0),)),
        (17, ((PASS_Y, 1, 1),)),
        (18, ((FWD_Y, 2, 0), (PAR, 0, 2, 0),)),
        (20, ((OWN, 1, 2, 1), (PASS_Y, 3, 1),)),
        (21, ((PAR, 1, 3, 0),)),
        (23, ((FWD_Y, 2, 1), (PAR, 0, 2, 1),)),
        (24, ((PASS_Y, 2, 0),)),
        (25, ((PAR, 1, 1, 1),)),
        (28, ((OWN, 1, 1, 1), (PAR, 1, 3, 1),)),
        (30, ((PASS_Y, 2, 1),)),
        (33, ((PAR, 1, 2, 0),)),
        (36, ((PAR, 1, 2, 1),)),
    ),
    3: (
        (4, ((CROSSF, 0), (CROSSF, 1), (OWN, 0, 1, 0), (OWN, 0, 3, 0), (FWD_Y, 0, 0), (OWN, 0, 1, 1), (OWN, 0, 3, 1), (FWD_Y, 0, 1), (OWN, 1, 0, 0), (OWN, 1, 0, 1), (OWN, 0, 2, 0), (FWD_Y, 1, 0), (OWN, 0, 2, 1), (PAR, 1, 0, 0), (PAR, 0, 0, 0),)),
        (6, ((OWN, 1, 1, 0), (FWD_Y, 3, 0),)),
        (7, ((OWN, 1, 3, 0),)),
        (8, ((PAR, 0, 0, 1), (PAR, 1, 0, 1),)),
        (10, ((OWN, 1, 1, 1), (FWD_Y, 1, 1),)),
        (11, ((OWN, 1, 3, 1),)),
        (12, ((PAR, 0, 1, 0), (PAR, 1, 1, 0),)),
        (14, ((FWD_Y, 3, 1),)),
        (16, ((PAR, 0, 3, 0), (PAR, 1, 3, 0),)),
        (18, ((OWN, 1, 2, 0), (FWD_Y, 2, 0),)),
        (20, ((PAR, 0, 1, 1), (PAR, 1, 1, 1),)),
        (23, ((FWD_Y, 2, 1),)),
        (24, ((PAR, 0, 3, 1), (PAR, 1, 3, 1),)),
        (28, ((PAR, 0, 2, 0), (PAR, 1, 2, 0),)),
        (33, ((PAR, 0, 2, 1), (PAR, 1, 2, 1),)),
        (34, ((OWN, 1, 2, 1),)),
    ),
}


def kernel(dims, mine, amps, out, own, par, rc, half, acc, t1, t2, t3, tc,
           ssem, own_sem, own_d, par_sem, par_d, t1_sem, t2_sem, t3_sem, tc_sem, cross_sem, local_sem):
    sym, tile, c = lax.axis_index("sym"), lax.axis_index("tile"), lax.axis_index("occ")
    x, yhi = sym % 4, sym // 4
    x0, x1 = x % 2, x // 2
    z, ylo = tile // 2, tile % 2
    z0, z1 = z % 2, z // 2
    y = 2 * yhi + ylo

    def dev(dx=0, dy=0, dz=0, dc=0):
        xx, yy, zz = (x + 4 + dx) % 4, (y + 4 + dy) % 4, (z + 4 + dz) % 4
        return {"sym": (yy // 2) * 4 + xx, "tile": zz * 2 + yy % 2, "occ": (c + dc) % 2}

    step_a = 1 - 2 * (yhi + ylo - 2 * yhi * ylo)
    step_z = 1 - 2 * z0
    to = {
        "x+": dev(dx=1), "x-": dev(dx=-1), "y+": dev(dy=1), "y-": dev(dy=-1), "z+": dev(dz=1), "z-": dev(dz=-1),
        "core": dev(dc=1), "ya": dev(dy=step_a), "yb": dev(dy=-step_a), "za": dev(dz=step_z), "zb": dev(dz=-step_z),
    }
    barrier = pltpu.get_barrier_semaphore()
    for name in ("x+", "x-", "y+", "y-", "z+", "z-", "core"):
        pl.semaphore_signal(barrier, inc=1, device_id=to[name], device_id_type=MESH)

    keep = pltpu.make_async_copy(mine, own.at[sym, c], local_sem.at[8])
    keep.start()
    loads = [pltpu.make_async_copy(amps.at[i], rc.at[:, pl.ds(i * V, V)], local_sem.at[i]) for i in range(NI)]
    for load in loads:
        load.start()

    hi, lo = yhi == 1, yhi == 0
    is_x = [x == k for k in range(4)]
    none = jnp.logical_and(x == 0, lo)
    row_of = {0: yhi, 1: 1 - yhi}
    name_of = {(row, j): row_of[row] * 4 + (x + 4 - j) % 4 for row in range(2) for j in range(4)}
    row_behind = {"+": ((y + 3) % 4) // 2, "-": ((y + 1) % 4) // 2}
    name_behind = {(sign, j): row_behind[sign] * 4 + (x + 4 - j) % 4 for sign in "+-" for j in range(4)}
    from_lo = {sign: row_behind[sign] == 0 for sign in "+-"}
    piece = [pl.ds(k * PV, PV) for k in range(PIECES)]
    pl.semaphore_wait(barrier, 7)

    sent = {None: [], 0: [], 1: [], 2: [], 3: []}

    def sign_of(j, k):
        return "+" if (k + (0, 1, 1, 0)[j]) % 2 == 0 else "-"

    def send(cls, make, cond=None):
        index = len(sent[None]) if cls is None else 12 + len(sent[cls])

        def copy():
            src, dst, where, recv = make()
            return pltpu.make_async_remote_copy(
                src, dst, ssem.at[index], recv, device_id=to[where], device_id_type=MESH
            )

        if cond is None:
            copy().start()
        else:
            pl.when(cond)(lambda: copy().start())
        sent[cls].append((cond, copy))

    def arrived(dst, recv, cond=None):
        def wait():
            pltpu.make_async_remote_copy(
                dst, dst, ssem.at[0], recv, device_id=to["core"], device_id_type=MESH
            ).wait_recv()

        if cond is None:
            wait()
        else:
            pl.when(cond)(wait)

    def unit(buffer, q, k):
        return buffer.at[q, c, piece[k]]

    def feed(cls, j, k, src):
        q = name_of[0, j]
        final = lambda where: lambda: (src(), unit(par, q, k), where, par_sem.at[q, k])
        via1 = lambda where: lambda: (src(), t1.at[j, piece[k]], where, t1_sem.at[j, k])
        via2 = lambda where: lambda: (src(), t2.at[j, piece[k]], where, t2_sem.at[j, k])
        if cls in (0, 1):
            send(cls, via1("z" + sign_of(j, k)))
        if cls == 1:
            send(cls, final("ya"))
        if cls == 2:
            send(cls, final("za"), lo)
            send(cls, via1("za"), hi)
            send(cls, via2("zb"), lo)
            send(cls, final("zb"), hi)
        if cls == 3:
            send(cls, via1("za"))
            send(cls, via2("zb"))

    def event(cls, kind, *args):
        if kind == CROSSF:
            (k,) = args
            sign = "+-"[k]
            arrived(tc.at[piece[k]], tc_sem.at[k])
            send(cls, lambda: (tc.at[piece[k]], own.at[row_behind[sign] * 4 + x, c, piece[k]], "y" + sign, cross_sem.at[k]))
        if kind == OWN:
            row, j, k = args
            q = name_of[row, j]
            here = lambda: unit(own, q, k)
            arrived(here(), cross_sem.at[k] if (row, j) == (1, 0) else own_sem.at[q, k])
            if (row, j) == (1, 0) or (j == 1 and (k + row) % 2 == 0):
                send(cls, lambda: (here(), here(), "x+", own_sem.at[q, k]))
            if (row, j) == (1, 0) or (j == 3 and (k + row) % 2 == 1):
                send(cls, lambda: (here(), here(), "x-", own_sem.at[q, k]))
            if row == 0:
                feed(cls, j, k, here)
            send(cls, lambda: (here(), here(), "core", own_d.at[q, k]))
        if kind == PASS_Z:
            j, k = args
            q = name_of[0, j]
            way = "z" + sign_of(j, k)
            here = lambda: t1.at[j, piece[k]]
            arrived(here(), t1_sem.at[j, k])
            on = lambda: (here(), t2.at[j, piece[k]], way, t2_sem.at[j, k])
            if cls == 1:
                send(cls, on)
            else:
                send(cls, on, lo)
                send(cls, lambda: (here(), unit(par, q, k), way, par_sem.at[q, k]), hi)
        if kind == FWD_Y:
            j, k = args
            q = name_of[0, j]
            way = "y" + sign_of(j, k)
            here1, here2 = (lambda: t1.at[j, piece[k]]), (lambda: t2.at[j, piece[k]])
            if cls in (2, 3):
                cond = None if cls == 3 else hi
                arrived(here1(), t1_sem.at[j, k], cond)
                if cls == 3:
                    send(cls, lambda: (here1(), unit(par, q, k), "ya", par_sem.at[q, k]))
                else:
                    send(cls, lambda: (here1(), t3.at[j, piece[k]], way, t3_sem.at[j, k]), hi)
            if cls in (1, 3):
                arrived(here2(), t2_sem.at[j, k])
                send(cls, lambda: (here2(), unit(par, q, k), "yb", par_sem.at[q, k]))
            else:
                arrived(here2(), t2_sem.at[j, k], lo)
                send(cls, lambda: (here2(), t3.at[j, piece[k]], way, t3_sem.at[j, k]), lo)
        if kind == PASS_Y:
            j, k = args
            sign = sign_of(j, k)
            q = name_behind[sign, j]
            cond = None if cls == 2 else from_lo[sign]
            arrived(t3.at[j, piece[k]], t3_sem.at[j, k], cond)
            send(cls, lambda: (t3.at[j, piece[k]], unit(par, q, k), "y" + sign, par_sem.at[q, k]), cond)
        if kind == PAR:
            row, j, k = args
            q = name_of[row, j]
            here = lambda: unit(par, q, k)
            cond = hi if cls == 0 else None
            arrived(here(), par_sem.at[q, k], cond)
            send(cls, lambda: (here(), here(), "core", par_d.at[q, k]), cond)

    def events(n):
        for cls in range(4):
            todo = dict(EVENTS[cls]).get(n, ())
            if todo:
                @pl.when(is_x[cls])
                def _():
                    for entry in todo:
                        event(cls, *entry)

    def events_within(base, m):
        for k in range(1, STEPS):
            if any(base + k in dict(EVENTS[cls]) for cls in range(4)):
                pl.when(m == k)(functools.partial(events, base + k))

    def first_stage(base, row, j):
        q = name_of[row, j]
        events(base)
        for k in range(PIECES):
            arrived(own.at[q, 1 - c, piece[k]], own_d.at[q, k])

        @pl.when(none)
        def _():
            pltpu.make_async_copy(own.at[q], par.at[q], local_sem.at[9 + q]).start()

        @pl.loop(0, STEPS)
        def _(m):
            events_within(base, m)
            for t in range(3):
                cols = pl.ds(pl.multiple_of(m * (2 * V) + t * 256, 256), 256)
                r = jnp.dot(own[q].reshape(2 * V, V), rc[:, cols], preferred_element_type=jnp.float32)
                r = r.astype(jnp.bfloat16)
                for lo_col, hi_col, pair, at in (((0, 256, 0, 0),), ((0, 128, 0, 256), (128, 256, 1, 0)), ((0, 256, 1, 128),))[t]:
                    rows = pl.ds(pl.multiple_of((2 * m + pair) * V, V), V)
                    for p in range(2):
                        lanes = pl.ds(p * V + at, hi_col - lo_col)
                        half[q, rows, lanes] = r[p * V:(p + 1) * V, lo_col:hi_col]

    def second_stage(base, row, j):
        q = name_of[row, j]
        events(base)
        for k in range(PIECES):
            arrived(par.at[q, 1 - c, piece[k]], par_d.at[q, k], jnp.logical_not(none))
        start, last = base == FIRST_SUM, base == STEPS * (len(SEQUENCE) - 1)

        @pl.when(none)
        def _():
            pltpu.make_async_copy(own.at[q], par.at[q], local_sem.at[9 + q]).wait()

        @pl.loop(0, STEPS)
        def _(m):
            events_within(base, m)
            rows = pl.ds(pl.multiple_of(m * (2 * V), 2 * V), 2 * V)
            for b0, b1 in ((0, 256), (256, 384)):
                right = jnp.concatenate([par[q, 0, b0:b1], par[q, 1, b0:b1]], axis=1)
                r = lax.dot_general(half[q, rows, :], right, (((1,), (1,)), ((), ())), preferred_element_type=jnp.float32)
                if start:
                    acc[rows, b0:b1] = r
                else:
                    acc[rows, b0:b1] += r
            if last:
                pltpu.make_async_copy(acc.at[rows], out.at[rows], local_sem.at[m]).start()

    for k in range(PIECES):
        src = mine.at[piece[k]]
        home = own.at[sym, c, piece[k]]
        send(None, lambda src=src, home=home, k=k: (src, home, "core", own_d.at[sym, k]))
    for k in range(PIECES):
        src = mine.at[piece[k]]
        home = own.at[sym, c, piece[k]]
        for way in ("x+", "x-"):
            send(None, lambda src=src, home=home, k=k, way=way: (src, home, way, own_sem.at[sym, k]))
        send(None, lambda src=src, k=k: (src, tc.at[piece[k]], "y" + "+-"[k], tc_sem.at[k]))
        for cls in range(4):
            @pl.when(is_x[cls])
            def _():
                feed(cls, 0, k, lambda src=src: src)

    n_row = dims[tile]
    n_col = dims[(z1 + yhi - 2 * z1 * yhi) * 4 + (z0 + x1 - 2 * z0 * x1) * 2 + (ylo + x0 - 2 * ylo * x0)]
    live_r = jnp.where(lax.broadcasted_iota(jnp.int32, (V, V), 0) < n_row, 1.0, 0.0)
    live = jnp.where(lax.broadcasted_iota(jnp.int32, (V, V), 1) < n_col, live_r, 0.0).astype(jnp.bfloat16)
    for load in loads:
        load.wait()
    for i in range(NI):
        rc[:, i * V:(i + 1) * V] = rc[:, i * V:(i + 1) * V] * live
    keep.wait()

    for number, (stage, row, j) in enumerate(SEQUENCE):
        (first_stage if stage == 1 else second_stage)(STEPS * number, row, j)
    events(STEPS * len(SEQUENCE))

    for cls, entries in sent.items():
        def finish(entries=entries):
            for cond, copy in entries:
                if cond is None:
                    copy().wait_send()
                else:
                    pl.when(cond)(lambda copy=copy: copy().wait_send())

        if cls is None:
            finish()
        else:
            pl.when(is_x[cls])(finish)
    for m in range(STEPS):
        rows = pl.ds(m * (2 * V), 2 * V)
        pltpu.make_async_copy(acc.at[rows], out.at[rows], local_sem.at[m]).wait()


FIRST_SUM = STEPS * [stage for stage, _, _ in SEQUENCE].index(2)


def mask_kernel(dims, raw, out):
    sym, tile = lax.axis_index("sym"), lax.axis_index("tile")
    n_row, n_col = dims[tile], dims[jnp.bitwise_xor(tile, sym)]
    live = (lax.broadcasted_iota(jnp.int32, (V, V), 0) < n_row) & (lax.broadcasted_iota(jnp.int32, (V, V), 1) < n_col)
    out[0, 0] = jnp.where(live, raw[...], 0.0)


def shards(irrep_dims, chol_vectors, amplitudes):
    bf, sem = jnp.bfloat16, pltpu.SemaphoreType.DMA
    raw = pl.pallas_call(
        kernel,
        out_shape=jax.ShapeDtypeStruct((NI * V, V), jnp.float32),
        in_specs=[
            pl.BlockSpec(memory_space=pltpu.SMEM),
            pl.BlockSpec(memory_space=pl.ANY),
            pl.BlockSpec(memory_space=pl.ANY),
        ],
        out_specs=pl.BlockSpec(memory_space=pl.ANY),
        scratch_shapes=[
            pltpu.VMEM((8, 2, V, V), bf),
            pltpu.VMEM((8, 2, V, V), bf),
            pltpu.VMEM((V, NI * V), bf),
            pltpu.VMEM((8, NI * V, 2 * V), bf),
            pltpu.VMEM((NI * V, V), jnp.float32),
            pltpu.VMEM((4, V, V), bf),
            pltpu.VMEM((4, V, V), bf),
            pltpu.VMEM((4, V, V), bf),
            pltpu.VMEM((V, V), bf),
            sem((136,)), sem((8, PIECES)), sem((8, PIECES)), sem((8, PIECES)), sem((8, PIECES)),
            sem((4, PIECES)), sem((4, PIECES)), sem((4, PIECES)), sem((2,)), sem((2,)), sem((17,)),
        ],
        compiler_params=pltpu.CompilerParams(
            collective_id=0, has_side_effects=True, vmem_limit_bytes=63 * 1024 * 1024
        ),
        cost_estimate=pl.CostEstimate(flops=29_000_000_000, bytes_accessed=7_500_000, transcendentals=0),
        name="ladder",
    )(irrep_dims, chol_vectors.reshape(V, V), amplitudes.reshape(NI, V, V))
    return pl.pallas_call(
        mask_kernel,
        grid=(NI,),
        out_shape=jax.ShapeDtypeStruct((1, NI, V, V), jnp.float32),
        in_specs=[pl.BlockSpec(memory_space=pltpu.SMEM), pl.BlockSpec((V, V), lambda i: (i, 0))],
        out_specs=pl.BlockSpec((1, 1, V, V), lambda i: (0, i, 0, 0)),
        name="live",
    )(irrep_dims, raw)


def solution(mesh):
    return jax.shard_map(
        shards,
        mesh=mesh,
        in_specs=(P(), P(("sym", "occ"), "tile", None), P("sym", "occ", "tile", None)),
        out_specs=P("sym", "occ", "tile", None),
        check_vma=False,
    )
```

profile of v0, /device:TPU:3, one launch (start us, length us, event | category | flops | bytes accessed | tf_op | source)
XLA Modules:
  0.0 85.7 jit_solution(9998651399173630059)
XLA Ops:
  0.0 78.7 %ladder.1.raw = f32[3072,384]{1,0:T(8,128)} custom-call(s32[8]{0:T(128)} %dims.3, bf16[384,384]{1,0:T(8,128)(2,1)} %bitcast.3, bf16[8,384,384]{2,1,0:T(8,128)(2,1)} %bitcast.2), custom_call_target="tpu_custom_call" | custom-call | flops 28999999488 | bytes 7500000 | tf_op jit(solution)/shard_map/ladder/pallas_call | solution.py:397
  78.7 7.0 %live.1 = f32[1,8,384,384]{3,2,1,0:T(8,128)} custom-call(s32[8]{0:T(128)} %dims.3, f32[3072,384]{1,0:T(8,128)} %ladder.1.raw), custom_call_target="tpu_custom_call" | custom-call | tf_op jit(solution)/shard_map/live/pallas_call | solution.py:425
where the time goes:
time: 86.8 us; the launch traced here: 85.7 us
  Pallas kernels  85.7 us (99%)
    pallas_call x1, Pallas kernels, shards(): pl.pallas_call(kernel, out_shape=jax.ShapeDtypeStruct((NI * V, V), jnp.fl...  78.7 us
    pallas_call x1, Pallas kernels, shards(): pl.pallas_call(mask_kernel, grid=(NI,), out_shape=jax.ShapeDtypeStruct((1...  6.97 us

commit v1 on v0

--- a/solution.py
+++ b/solution.py
@@ -13,113 +13,113 @@
 PIECES = 2
 PV = V // PIECES
 STEPS = 4
+COLUMNS = (((0, 256, 0, 0),), ((0, 128, 0, 256), (128, 256, 1, 0)), ((0, 256, 1, 128),))
 CROSSF, OWN, PASS_Z, FWD_Y, PASS_Y, PAR = range(6)
 SEQUENCE = (
     (1, 0, 0),
+    (1, 0, 1),
     (1, 0, 2),
     (1, 0, 3),
-    (1, 0, 1),
     (2, 0, 0),
     (1, 1, 0),
+    (2, 0, 1),
     (2, 1, 0),
-    (1, 1, 1),
-    (1, 1, 3),
     (2, 0, 3),
-    (2, 0, 1),
-    (2, 1, 1),
-    (2, 1, 3),
     (2, 0, 2),
-    (1, 1, 2),
-    (2, 1, 2),
 )
 EVENTS = {
     0: (
-        (4, ((CROSSF, 0), (CROSSF, 1), (OWN, 0, 1, 0), (OWN, 0, 3, 0), (PASS_Z, 0, 0), (PASS_Z, 0, 1), (OWN, 0, 1, 1), (OWN, 0, 3, 1), (OWN, 1, 0, 0), (OWN, 1, 0, 1), (PASS_Z, 1, 0), (PASS_Z, 3, 0), (OWN, 0, 2, 0), (OWN, 0, 2, 1), (FWD_Y, 0, 1), (PAR, 0, 0, 1), (FWD_Y, 0, 0), (PAR, 0, 0, 0),)),
-        (6, ((OWN, 1, 1, 0),)),
-        (8, ((PASS_Z, 1, 1), (PASS_Z, 3, 1),)),
-        (9, ((PASS_Y, 0, 1), (PASS_Y, 0, 0),)),
-        (10, ((OWN, 1, 1, 1),)),
-        (12, ((OWN, 1, 3, 0), (FWD_Y, 1, 0), (FWD_Y, 3, 0), (PAR, 0, 1, 0), (PAR, 0, 3, 0),)),
-        (15, ((PAR, 1, 0, 0), (PAR, 1, 0, 1),)),
-        (16, ((OWN, 1, 2, 1), (PASS_Z, 2, 0), (PASS_Z, 2, 1),)),
-        (19, ((PASS_Y, 1, 0), (PASS_Y, 3, 0),)),
-        (20, ((OWN, 1, 2, 0), (FWD_Y, 1, 1), (FWD_Y, 3, 1), (PAR, 0, 1, 1), (PAR, 0, 3, 1),)),
-        (25, ((FWD_Y, 2, 0), (FWD_Y, 2, 1), (PAR, 0, 2, 0), (PAR, 0, 2, 1), (PAR, 1, 3, 0), (PAR, 1, 1, 0),)),
-        (28, ((OWN, 1, 3, 1), (PASS_Y, 3, 1), (PASS_Y, 1, 1),)),
-        (33, ((PASS_Y, 2, 0), (PASS_Y, 2, 1),)),
-        (37, ((PAR, 1, 3, 1), (PAR, 1, 1, 1),)),
-        (41, ((PAR, 1, 2, 0), (PAR, 1, 2, 1),)),
+        (3, ((CROSSF, 0), (OWN, 0, 1, 0), (OWN, 0, 3, 0), (PASS_Z, 0, 0),)),
+        (4, ((CROSSF, 1), (PASS_Z, 0, 1), (OWN, 0, 1, 1), (OWN, 0, 3, 1), (OWN, 1, 0, 0), (PASS_Z, 1, 0),)),
+        (5, ((PASS_Z, 3, 0),)),
+        (6, ((OWN, 1, 0, 1),)),
+        (7, ((OWN, 0, 2, 0),)),
+        (8, ((OWN, 0, 2, 1), (FWD_Y, 0, 0), (PAR, 0, 0, 0), (FWD_Y, 0, 1), (PAR, 0, 0, 1),)),
+        (9, ((OWN, 1, 1, 0),)),
+        (10, ((PASS_Z, 1, 1), (PASS_Z, 3, 1),)),
+        (12, ((OWN, 1, 1, 1), (PASS_Y, 0, 1), (PASS_Y, 0, 0),)),
+        (13, ((OWN, 1, 3, 0), (FWD_Y, 1, 0), (FWD_Y, 3, 0), (PAR, 0, 1, 0), (PAR, 0, 3, 0),)),
+        (17, ((OWN, 1, 2, 0), (OWN, 1, 2, 1), (PASS_Z, 2, 0), (PASS_Z, 2, 1), (PAR, 1, 0, 0), (PAR, 1, 0, 1),)),
+        (20, ((FWD_Y, 1, 1), (FWD_Y, 3, 1), (PASS_Y, 1, 0), (PASS_Y, 3, 0), (PAR, 0, 1, 1), (PAR, 0, 3, 1),)),
+        (24, ((FWD_Y, 2, 0), (FWD_Y, 2, 1), (PAR, 0, 2, 0), (PAR, 0, 2, 1),)),
+        (25, ((PAR, 1, 3, 0), (PAR, 1, 1, 0),)),
+        (27, ((OWN, 1, 3, 1), (PASS_Y, 3, 1), (PASS_Y, 1, 1),)),
+        (31, ((PASS_Y, 2, 0), (PASS_Y, 2, 1),)),
+        (34, ((PAR, 1, 3, 1), (PAR, 1, 1, 1),)),
+        (38, ((PAR, 1, 2, 0), (PAR, 1, 2, 1),)),
     ),
     1: (
-        (4, ((CROSSF, 0), (OWN, 0, 1, 0), (OWN, 0, 3, 0), (PASS_Z, 0, 0), (PASS_Z, 0, 1), (OWN, 0, 1, 1), (OWN, 0, 3, 1), (CROSSF, 1), (PASS_Z, 1, 0), (PASS_Z, 3, 0), (OWN, 0, 2, 0), (OWN, 0, 2, 1), (FWD_Y, 0, 1), (FWD_Y, 0, 0),)),
-        (5, ((OWN, 1, 0, 0),)),
-        (6, ((OWN, 1, 1, 0),)),
-        (7, ((OWN, 1, 3, 0),)),
-        (8, ((PASS_Z, 1, 1), (PASS_Z, 3, 1),)),
-        (9, ((PAR, 0, 0, 1), (PAR, 1, 0, 1),)),
-        (10, ((OWN, 1, 1, 1),)),
-        (11, ((OWN, 1, 3, 1),)),
-        (12, ((FWD_Y, 1, 0), (FWD_Y, 3, 0),)),
-        (13, ((PAR, 0, 0, 0), (PAR, 1, 0, 0),)),
-        (15, ((OWN, 1, 2, 0),)),
-        (16, ((OWN, 1, 2, 1), (PASS_Z, 2, 0), (PASS_Z, 2, 1),)),
+        (3, ((CROSSF, 0), (OWN, 0, 1, 0), (OWN, 0, 3, 0), (PASS_Z, 0, 0),)),
+        (4, ((PASS_Z, 0, 1), (OWN, 0, 1, 1), (OWN, 0, 3, 1), (CROSSF, 1), (PASS_Z, 1, 0),)),
+        (5, ((PASS_Z, 3, 0),)),
+        (7, ((OWN, 0, 2, 0),)),
+        (8, ((OWN, 0, 2, 1), (FWD_Y, 0, 0), (FWD_Y, 0, 1), (OWN, 1, 0, 0),)),
+        (9, ((OWN, 1, 1, 0),)),
+        (10, ((OWN, 1, 3, 0), (PASS_Z, 1, 1), (PASS_Z, 3, 1),)),
+        (12, ((PAR, 0, 0, 0), (PAR, 1, 0, 0), (OWN, 1, 1, 1),)),
+        (13, ((OWN, 1, 3, 1), (FWD_Y, 1, 0), (FWD_Y, 3, 0),)),
+        (15, ((PAR, 0, 0, 1), (PAR, 1, 0, 1),)),
+        (16, ((OWN, 1, 2, 0), (PASS_Z, 2, 0),)),
+        (17, ((PASS_Z, 2, 1), (OWN, 1, 2, 1),)),
         (18, ((PAR, 0, 1, 0), (PAR, 1, 1, 0),)),
         (20, ((FWD_Y, 1, 1), (FWD_Y, 3, 1), (OWN, 1, 0, 1),)),
         (22, ((PAR, 0, 3, 0), (PAR, 1, 3, 0),)),
-        (24, ((FWD_Y, 2, 0), (FWD_Y, 2, 1),)),
-        (26, ((PAR, 0, 1, 1), (PAR, 1, 1, 1),)),
-        (30, ((PAR, 1, 3, 1),)),
-        (31, ((PAR, 0, 3, 1),)),
-        (35, ((PAR, 0, 2, 0), (PAR, 1, 2, 0),)),
-        (39, ((PAR, 0, 2, 1), (PAR, 1, 2, 1),)),
+        (23, ((FWD_Y, 2, 0), (FWD_Y, 2, 1),)),
+        (24, ((PAR, 0, 1, 1), (PAR, 1, 1, 1),)),
+        (27, ((PAR, 0, 3, 1), (PAR, 1, 3, 1),)),
+        (30, ((PAR, 0, 2, 0), (PAR, 1, 2, 0),)),
+        (34, ((PAR, 0, 2, 1), (PAR, 1, 2, 1),)),
     ),
     2: (
-        (4, ((CROSSF, 0), (CROSSF, 1), (OWN, 0, 1, 0), (OWN, 0, 3, 0), (FWD_Y, 0, 0), (PAR, 0, 0, 0), (OWN, 0, 1, 1), (OWN, 0, 3, 1), (PAR, 0, 0, 1), (FWD_Y, 0, 1), (OWN, 1, 0, 0), (OWN, 1, 0, 1), (OWN, 0, 2, 0), (PAR, 0, 1, 0), (FWD_Y, 1, 0), (OWN, 0, 2, 1), (PASS_Y, 0, 0), (PASS_Y, 0, 1),)),
-        (6, ((FWD_Y, 3, 0), (PAR, 0, 3, 0),)),
-        (7, ((OWN, 1, 3, 0),)),
-        (8, ((PASS_Y, 1, 0),)),
-        (9, ((PAR, 1, 0, 0),)),
-        (10, ((FWD_Y, 1, 1), (PAR, 0, 1, 1),)),
-        (11, ((OWN, 1, 1, 0), (OWN, 1, 3, 1),)),
-        (12, ((PAR, 1, 0, 1),)),
-        (13, ((PASS_Y, 3, 0),)),
-        (14, ((FWD_Y, 3, 1), (PAR, 0, 3, 1),)),
-        (15, ((OWN, 1, 2, 0),)),
-        (16, ((PAR, 1, 1, 0),)),
-        (17, ((PASS_Y, 1, 1),)),
-        (18, ((FWD_Y, 2, 0), (PAR, 0, 2, 0),)),
-        (20, ((OWN, 1, 2, 1), (PASS_Y, 3, 1),)),
-        (21, ((PAR, 1, 3, 0),)),
-        (23, ((FWD_Y, 2, 1), (PAR, 0, 2, 1),)),
-        (24, ((PASS_Y, 2, 0),)),
-        (25, ((PAR, 1, 1, 1),)),
-        (28, ((OWN, 1, 1, 1), (PAR, 1, 3, 1),)),
-        (30, ((PASS_Y, 2, 1),)),
-        (33, ((PAR, 1, 2, 0),)),
-        (36, ((PAR, 1, 2, 1),)),
+        (3, ((CROSSF, 0), (OWN, 0, 1, 0), (OWN, 0, 3, 0), (FWD_Y, 0, 0), (PAR, 0, 0, 0),)),
+        (4, ((CROSSF, 1), (OWN, 0, 1, 1), (OWN, 0, 3, 1), (PAR, 0, 0, 1), (FWD_Y, 0, 1), (OWN, 1, 0, 0),)),
+        (6, ((OWN, 1, 0, 1),)),
+        (7, ((OWN, 0, 2, 0), (FWD_Y, 1, 0), (PAR, 0, 1, 0),)),
+        (8, ((OWN, 0, 2, 1), (PASS_Y, 0, 0), (PASS_Y, 0, 1),)),
+        (9, ((FWD_Y, 3, 0), (PAR, 0, 3, 0),)),
+        (10, ((OWN, 1, 3, 0),)),
+        (11, ((PASS_Y, 1, 0),)),
+        (12, ((FWD_Y, 1, 1), (PAR, 0, 1, 1), (PAR, 1, 0, 0),)),
+        (13, ((OWN, 1, 1, 0), (OWN, 1, 3, 1),)),
+        (14, ((PAR, 1, 0, 1),)),
+        (15, ((FWD_Y, 3, 1), (PASS_Y, 3, 0), (PAR, 0, 3, 1),)),
+        (16, ((OWN, 1, 2, 0),)),
+        (17, ((OWN, 1, 2, 1),)),
+        (18, ((PASS_Y, 1, 1), (PAR, 1, 1, 0),)),
+        (19, ((FWD_Y, 2, 0), (PAR, 0, 2, 0),)),
+        (21, ((PASS_Y, 3, 1),)),
+        (22, ((FWD_Y, 2, 1), (PAR, 0, 2, 1), (PAR, 1, 3, 0),)),
+        (25, ((PASS_Y, 2, 0), (PAR, 1, 1, 1),)),
+        (27, ((OWN, 1, 1, 1),)),
+        (28, ((PAR, 1, 3, 1),)),
+        (29, ((PASS_Y, 2, 1),)),
+        (31, ((PAR, 1, 2, 0),)),
+        (34, ((PAR, 1, 2, 1),)),
     ),
     3: (
-        (4, ((CROSSF, 0), (CROSSF, 1), (OWN, 0, 1, 0), (OWN, 0, 3, 0), (FWD_Y, 0, 0), (OWN, 0, 1, 1), (OWN, 0, 3, 1), (FWD_Y, 0, 1), (OWN, 1, 0, 0), (OWN, 1, 0, 1), (OWN, 0, 2, 0), (FWD_Y, 1, 0), (OWN, 0, 2, 1), (PAR, 1, 0, 0), (PAR, 0, 0, 0),)),
-        (6, ((OWN, 1, 1, 0), (FWD_Y, 3, 0),)),
-        (7, ((OWN, 1, 3, 0),)),
-        (8, ((PAR, 0, 0, 1), (PAR, 1, 0, 1),)),
-        (10, ((OWN, 1, 1, 1), (FWD_Y, 1, 1),)),
-        (11, ((OWN, 1, 3, 1),)),
-        (12, ((PAR, 0, 1, 0), (PAR, 1, 1, 0),)),
-        (14, ((FWD_Y, 3, 1),)),
-        (16, ((PAR, 0, 3, 0), (PAR, 1, 3, 0),)),
-        (18, ((OWN, 1, 2, 0), (FWD_Y, 2, 0),)),
+        (3, ((CROSSF, 0), (OWN, 0, 1, 0), (OWN, 0, 3, 0), (FWD_Y, 0, 0),)),
+        (4, ((CROSSF, 1), (OWN, 0, 1, 1), (OWN, 0, 3, 1), (FWD_Y, 0, 1), (OWN, 1, 0, 0),)),
+        (7, ((OWN, 0, 2, 0), (FWD_Y, 1, 0),)),
+        (8, ((OWN, 0, 2, 1), (OWN, 1, 0, 1), (PAR, 0, 0, 0), (PAR, 1, 0, 0),)),
+        (9, ((OWN, 1, 1, 0), (FWD_Y, 3, 0),)),
+        (10, ((OWN, 1, 3, 0), (PAR, 0, 0, 1), (PAR, 1, 0, 1),)),
+        (12, ((OWN, 1, 1, 1), (FWD_Y, 1, 1),)),
+        (13, ((OWN, 1, 3, 1), (PAR, 0, 1, 0), (PAR, 1, 1, 0),)),
+        (15, ((FWD_Y, 3, 1),)),
+        (17, ((PAR, 1, 3, 0), (PAR, 0, 3, 0),)),
+        (18, ((OWN, 1, 2, 0),)),
+        (19, ((FWD_Y, 2, 0),)),
         (20, ((PAR, 0, 1, 1), (PAR, 1, 1, 1),)),
-        (23, ((FWD_Y, 2, 1),)),
-        (24, ((PAR, 0, 3, 1), (PAR, 1, 3, 1),)),
-        (28, ((PAR, 0, 2, 0), (PAR, 1, 2, 0),)),
-        (33, ((PAR, 0, 2, 1), (PAR, 1, 2, 1),)),
-        (34, ((OWN, 1, 2, 1),)),
+        (22, ((FWD_Y, 2, 1),)),
+        (24, ((PAR, 1, 3, 1), (PAR, 0, 3, 1),)),
+        (27, ((PAR, 0, 2, 0), (PAR, 1, 2, 0),)),
+        (31, ((PAR, 1, 2, 1), (PAR, 0, 2, 1),)),
+        (32, ((OWN, 1, 2, 1),)),
     ),
 }
 
 
-def kernel(dims, mine, amps, out, own, par, rc, half, acc, t1, t2, t3, tc,
+def kernel(dims, mine, amps, out, out_own, out_par, own, par, rc, half, acc, t1, t2, t3, tc,
            ssem, own_sem, own_d, par_sem, par_d, t1_sem, t2_sem, t3_sem, tc_sem, cross_sem, local_sem):
     sym, tile, c = lax.axis_index("sym"), lax.axis_index("tile"), lax.axis_index("occ")
     x, yhi = sym % 4, sym // 4
@@ -305,7 +305,7 @@
                 cols = pl.ds(pl.multiple_of(m * (2 * V) + t * 256, 256), 256)
                 r = jnp.dot(own[q].reshape(2 * V, V), rc[:, cols], preferred_element_type=jnp.float32)
                 r = r.astype(jnp.bfloat16)
-                for lo_col, hi_col, pair, at in (((0, 256, 0, 0),), ((0, 128, 0, 256), (128, 256, 1, 0)), ((0, 256, 1, 128),))[t]:
+                for lo_col, hi_col, pair, at in COLUMNS[t]:
                     rows = pl.ds(pl.multiple_of((2 * m + pair) * V, V), V)
                     for p in range(2):
                         lanes = pl.ds(p * V + at, hi_col - lo_col)
@@ -365,6 +365,25 @@
         (first_stage if stage == 1 else second_stage)(STEPS * number, row, j)
     events(STEPS * len(SEQUENCE))
 
+    leaving = []
+    for r, (row, j) in enumerate(REST):
+        q = name_of[row, j]
+        for k in range(PIECES):
+            arrived(own.at[q, 1 - c, piece[k]], own_d.at[q, k])
+        for k in range(PIECES):
+            arrived(par.at[q, 1 - c, piece[k]], par_d.at[q, k], jnp.logical_not(none))
+        leaving.append(pltpu.make_async_copy(own.at[q], out_own.at[r], local_sem.at[17 + 2 * r]))
+        leaving[-1].start()
+        leaving.append(pltpu.make_async_copy(par.at[q], out_par.at[r], local_sem.at[18 + 2 * r]))
+
+        @pl.when(none)
+        def _():
+            pltpu.make_async_copy(own.at[q], out_par.at[r], local_sem.at[18 + 2 * r]).start()
+
+        @pl.when(jnp.logical_not(none))
+        def _():
+            leaving[-1].start()
+
     for cls, entries in sent.items():
         def finish(entries=entries):
             for cond, copy in entries:
@@ -380,29 +399,50 @@
     for m in range(STEPS):
         rows = pl.ds(m * (2 * V), 2 * V)
         pltpu.make_async_copy(acc.at[rows], out.at[rows], local_sem.at[m]).wait()
-
-
+    for copy in leaving:
+        copy.wait()
+
+
+REST = tuple((row, j) for j in (0, 1, 3, 2) for row in range(2) if (1, row, j) not in SEQUENCE)
 FIRST_SUM = STEPS * [stage for stage, _, _ in SEQUENCE].index(2)
 
 
-def mask_kernel(dims, raw, out):
+def rest_kernel(dims, own, par, amps, raw, out, rc, half):
     sym, tile = lax.axis_index("sym"), lax.axis_index("tile")
     n_row, n_col = dims[tile], dims[jnp.bitwise_xor(tile, sym)]
     live = (lax.broadcasted_iota(jnp.int32, (V, V), 0) < n_row) & (lax.broadcasted_iota(jnp.int32, (V, V), 1) < n_col)
-    out[0, 0] = jnp.where(live, raw[...], 0.0)
+    live_b = jnp.where(live, 1.0, 0.0).astype(jnp.bfloat16)
+    for i in range(2):
+        rc[:, i * V:(i + 1) * V] = amps[i] * live_b
+    n = len(REST)
+    for t in range(3):
+        r = jnp.dot(own[...].reshape(n * 2 * V, V), rc[:, t * 256:(t + 1) * 256], preferred_element_type=jnp.float32)
+        r = r.astype(jnp.bfloat16)
+        for lo_col, hi_col, pair, at in COLUMNS[t]:
+            for p in range(2 * n):
+                lanes = pl.ds(p * V + at, hi_col - lo_col)
+                half[pair * V:(pair + 1) * V, lanes] = r[p * V:(p + 1) * V, lo_col:hi_col]
+    for b0, b1 in ((0, 256), (256, 384)):
+        right = jnp.concatenate([par[r, p, b0:b1] for r in range(n) for p in range(2)], axis=1)
+        r = lax.dot_general(half[...], right, (((1,), (1,)), ((), ())), preferred_element_type=jnp.float32)
+        r = r + raw[:, b0:b1]
+        for i in range(2):
+            out[0, i, :, b0:b1] = jnp.where(live[:, b0:b1], r[i * V:(i + 1) * V], 0.0)
 
 
 def shards(irrep_dims, chol_vectors, amplitudes):
     bf, sem = jnp.bfloat16, pltpu.SemaphoreType.DMA
-    raw = pl.pallas_call(
+    n = len(REST)
+    own, chol, amps = (n, 2, V, V), chol_vectors.reshape(V, V), amplitudes.reshape(NI, V, V)
+    raw, rest_own, rest_par = pl.pallas_call(
         kernel,
-        out_shape=jax.ShapeDtypeStruct((NI * V, V), jnp.float32),
+        out_shape=[jax.ShapeDtypeStruct((NI * V, V), jnp.float32), jax.ShapeDtypeStruct(own, bf), jax.ShapeDtypeStruct(own, bf)],
         in_specs=[
             pl.BlockSpec(memory_space=pltpu.SMEM),
             pl.BlockSpec(memory_space=pl.ANY),
             pl.BlockSpec(memory_space=pl.ANY),
         ],
-        out_specs=pl.BlockSpec(memory_space=pl.ANY),
+        out_specs=[pl.BlockSpec(memory_space=pl.ANY)] * 3,
         scratch_shapes=[
             pltpu.VMEM((8, 2, V, V), bf),
             pltpu.VMEM((8, 2, V, V), bf),
@@ -414,22 +454,31 @@
             pltpu.VMEM((4, V, V), bf),
             pltpu.VMEM((V, V), bf),
             sem((136,)), sem((8, PIECES)), sem((8, PIECES)), sem((8, PIECES)), sem((8, PIECES)),
-            sem((4, PIECES)), sem((4, PIECES)), sem((4, PIECES)), sem((2,)), sem((2,)), sem((17,)),
+            sem((4, PIECES)), sem((4, PIECES)), sem((4, PIECES)), sem((2,)), sem((2,)), sem((17 + 2 * n,)),
         ],
         compiler_params=pltpu.CompilerParams(
             collective_id=0, has_side_effects=True, vmem_limit_bytes=63 * 1024 * 1024
         ),
         cost_estimate=pl.CostEstimate(flops=29_000_000_000, bytes_accessed=7_500_000, transcendentals=0),
         name="ladder",
-    )(irrep_dims, chol_vectors.reshape(V, V), amplitudes.reshape(NI, V, V))
+    )(irrep_dims, chol, amps)
+    whole = pl.BlockSpec(own, lambda m: (0, 0, 0, 0), pipeline_mode=pl.Buffered(1))
     return pl.pallas_call(
-        mask_kernel,
-        grid=(NI,),
+        rest_kernel,
+        grid=(STEPS,),
         out_shape=jax.ShapeDtypeStruct((1, NI, V, V), jnp.float32),
-        in_specs=[pl.BlockSpec(memory_space=pltpu.SMEM), pl.BlockSpec((V, V), lambda i: (i, 0))],
-        out_specs=pl.BlockSpec((1, 1, V, V), lambda i: (0, i, 0, 0)),
-        name="live",
-    )(irrep_dims, raw)
+        in_specs=[
+            pl.BlockSpec(memory_space=pltpu.SMEM),
+            whole,
+            whole,
+            pl.BlockSpec((2, V, V), lambda m: (m, 0, 0)),
+            pl.BlockSpec((2 * V, V), lambda m: (m, 0)),
+        ],
+        out_specs=pl.BlockSpec((1, 2, V, V), lambda m: (0, m, 0, 0)),
+        scratch_shapes=[pltpu.VMEM((V, 2 * V), bf), pltpu.VMEM((2 * V, n * 2 * V), bf)],
+        compiler_params=pltpu.CompilerParams(vmem_limit_bytes=60 * 1024 * 1024),
+        name="rest",
+    )(irrep_dims, rest_own, rest_par, amps, raw)
 
 
 def solution(mesh):

time: 86.8 us -> 79.9 us (0.921)
  the two profiles are of different devices: /device:TPU:3 before, /device:TPU:25 now
where the time goes in v1:
time: 79.9 us; the launch traced here: 79.7 us
  Pallas kernels  79.7 us (100%)
    pallas_call x1, Pallas kernels, shards(): pl.pallas_call(kernel, out_shape=[jax.ShapeDtypeStruct((NI * V, V), jnp.f...  60.4 us
    pallas_call x1, Pallas kernels, shards(): pl.pallas_call(rest_kernel, grid=(STEPS,), out_shape=jax.ShapeDtypeStruct...  19.4 us

profile of v1, /device:TPU:25, one launch (start us, length us, event | category | flops | bytes accessed | tf_op | source)
XLA Modules:
  0.0 79.7 jit_solution(4274077151170940472)
XLA Ops:
  0.0 60.4 %ladder.1 = (f32[3072,384]{1,0:T(8,128)}, bf16[3,2,384,384]{3,2,1,0:T(8,128)(2,1)}, bf16[3,2,384,384]{3,2,1,0:T(8,128)(2,1)}) custom-call(s32[8]{0:T(128)} %dims.3, bf16[384,384]{1,0:T(8,128)(2,1)} %bitcast.4, bf16[8,384,384]{2,1,0:T(8,128)(2,1)} %bitcast.2), custom_call_target="tpu_custom_call" | custom-call | flops 28999999488 | bytes 7500000 | tf_op jit(solution)/shard_map/ladder/pallas_call | solution.py:437
  60.4 19.4 %rest.1 = f32[1,8,384,384]{3,2,1,0:T(8,128)} custom-call(s32[8]{0:T(128)} %dims.3, bf16[3,2,384,384]{3,2,1,0:T(8,128)(2,1)} %get-tuple-element.8.own, bf16[3,2,384,384]{3,2,1,0:T(8,128)(2,1)} %get-tuple-element.9.par, bf16[8,384,384]{2,1,0:T(8,128)(2,1)} %bitcast.3, f32[3072,384]{1,0:T(8,128)} %get-tuple-element.10.raw), custom_call_target="tpu_custom_call" | custom-call | tf_op jit(solution)/shard_map/rest/pallas_call | solution.py:466
